TPU v7x, 32 devices: a whole 2x2x4 slice. The times are simulated.
32 devices in a mesh: seq: 4 (over y, x), bat: 8 (over z, core).
Axes of the slice: x: 2, y: 2, z: 4, core: 2. Of those that a mesh axis runs over, the one named last changes fastest.
Arguments:
- block_input: float32 [8, 2048, 1024], P('bat', 'seq'), may hold values from -6 to 6
- cotangent: float32 [8, 2048, 1024], P('bat', 'seq'), may hold values from -6 to 6
- lengths: int32 [8], P('bat'), may hold values from 1537 to 2048, as said below
- norm_gains: float32 [2, 1024], replicated, may hold values from 0.5 to 1.5
- chan_params: float32 [8, 1536], replicated, may hold values from -3 to 12, as said below
- gate_blocks: float32 [2, 8, 192, 192], replicated, may hold values from -0.4375 to 0.4375
- gains_first: float32 [2, 1024], replicated, may hold values from -24 to 24
- gains_second: float32 [2, 1024], replicated, may hold values from 39.3216 to 622.592
- chan_first: float32 [8, 1536], replicated, may hold values from -448 to 448
- chan_second: float32 [8, 1536], replicated, may hold values from 4096 to 131072
- gate_first: float32 [2, 8, 192, 192], replicated, may hold values from -24 to 24
- gate_second: float32 [2, 8, 192, 192], replicated, may hold values from 39.3216 to 622.592
- tile_weights: float32 [3456, 32, 128], P(('seq', 'bat')), may hold values from -0.1875 to 0.1875
- tile_first: float32 [3456, 32, 128], P(('seq', 'bat')), may hold values from -24 to 24
- tile_second: float32 [3456, 32, 128], P(('seq', 'bat')), may hold values from 39.3216 to 622.592
- basis_left: float32 [3456, 32, 32], P(('seq', 'bat')), may hold values from -1 to 1, as said below
- basis_right: float32 [3456, 128, 128], P(('seq', 'bat')), may hold values from -1 to 1, as said below
- stat_left: float32 [3456, 32, 32], P(('seq', 'bat')), may hold values from -2097152 to 2097152, as said below
- stat_right: float32 [3456, 128, 128], P(('seq', 'bat')), may hold values from -2097152 to 2097152, as said below
- tile_of_slot: int32 [3456], replicated, may hold values from 0 to 3455, each once
Outputs:
- block_output: float32 [8, 2048, 1024], P('bat', 'seq')
- input_grad: float32 [8, 2048, 1024], P('bat', 'seq')
- gains_first_new: float32 [2, 1024], replicated
- gains_second_new: float32 [2, 1024], replicated
- gains_new: float32 [2, 1024], replicated
- chan_first_new: float32 [8, 1536], replicated
- chan_second_new: float32 [8, 1536], replicated
- chan_new: float32 [8, 1536], replicated
- gate_first_new: float32 [2, 8, 192, 192], replicated
- gate_second_new: float32 [2, 8, 192, 192], replicated
- gate_new: float32 [2, 8, 192, 192], replicated
- tile_first_new: float32 [3456, 32, 128], P(('seq', 'bat'))
- tile_second_new: float32 [3456, 32, 128], P(('seq', 'bat'))
- tile_weights_new: float32 [3456, 32, 128], P(('seq', 'bat'))
- basis_left_new: float32 [3456, 32, 32], P(('seq', 'bat'))
- basis_right_new: float32 [3456, 128, 128], P(('seq', 'bat'))
- stat_left_new: float32 [3456, 32, 32], P(('seq', 'bat'))
- stat_right_new: float32 [3456, 128, 128], P(('seq', 'bat'))
Inputs may be any that keep to these rules, and one draw needn't show every extreme that they name: `lengths`: every sequence has at least 1537 tokens; some sequence has exactly 2048. `tile_of_slot`: a permutation of the tile numbers. `chan_params`: the decay parameters of row 7 lie between 3.5 and 12. `basis_left`: each matrix is orthogonal. `basis_right`: each matrix is orthogonal. `stat_left`: each matrix is symmetric positive definite. `stat_right`: each matrix is symmetric positive definite.
All inputs are finite; a program needn't handle non-finite values.
Results may differ from a plain program's by a relative error of at most 0.008.
The roundings to bfloat16 on the way count: a program that leaves them out, or rounds other values in their place, can miss the bound.
Values may be sent and summed in bfloat16 or wider, within the bound.
A program may use at most 448 MiB of HBM per device.

v0:
```python
import jax
import jax.numpy as jnp
from jax import lax
from jax.sharding import PartitionSpec as P

D = 1024
R = 1536
F = 3072
HB = 8
CONV = 4
TI = 32
TO = 128
STEPNUM = 10
BS = 192


highest = lax.Precision.HIGHEST
norm_eps = 1e-06
beta_one = 0.9
beta_two = 0.95
adam_eps = 1e-08
learn_rate = 0.02
small_rate = 0.5
decay_rate = 0.01
decay_scale = 8.0


def entering(part, axis, combine, identity, reverse):
    count = lax.axis_size(axis)
    place = lax.axis_index(axis)
    ahead = count - 1 - place if reverse else place
    gathered = jax.tree.map(lambda a: lax.all_gather(a, axis), part)
    state = jax.tree.map(lambda a, e: jnp.zeros_like(a) + jnp.asarray(e, a.dtype), part, identity)

    def one(step, state):
        source = count - 1 - step if reverse else step
        return combine(
            state, jax.tree.map(lambda a: lax.dynamic_index_in_dim(a, source, 0, False), gathered)
        )

    return lax.fori_loop(0, ahead, one, state)


def passed_along(value, axis, by):
    devices = lax.axis_size(axis)
    pairs = [(i, i + by) for i in range(devices) if 0 <= i + by < devices]
    return lax.ppermute(value, axis, pairs)


def multiply(left_side, matrix):
    return jnp.dot(left_side, matrix, preferred_element_type=jnp.float32)


def multiply_transposed(left_side, matrix):
    return jnp.einsum("tj,ij->ti", left_side, matrix, preferred_element_type=jnp.float32)


def contract_rows(left_side, right_side):
    return jnp.einsum("ti,tj->ij", left_side, right_side, preferred_element_type=jnp.float32)


def rms_norm(values, gain_row):
    return (
        values * lax.rsqrt(jnp.mean(values * values, axis=-1, keepdims=True) + norm_eps) * gain_row
    )


def block_apply(values_low, blocks_low):
    token_count = values_low.shape[0]
    split_view = values_low.reshape(token_count, HB, BS)
    return jnp.einsum(
        "tbi,bij->tbj", split_view, blocks_low, preferred_element_type=jnp.float32
    ).reshape(token_count, R)


def block_back(grads_low, blocks_low):
    token_count = grads_low.shape[0]
    split_view = grads_low.reshape(token_count, HB, BS)
    return jnp.einsum(
        "tbj,bij->tbi", split_view, blocks_low, preferred_element_type=jnp.float32
    ).reshape(token_count, R)


def block_weight_grad(values_low, grads_low):
    token_count = values_low.shape[0]
    return jnp.einsum(
        "tbi,tbj->bij",
        values_low.reshape(token_count, HB, BS),
        grads_low.reshape(token_count, HB, BS),
        preferred_element_type=jnp.float32,
    )


def gate_piece(mix_keep, mix_admit, conv_out, bias_keep, bias_admit, lambda_row):
    keep_gate = jax.nn.sigmoid(mix_keep + bias_keep)
    admit_gate = jax.nn.sigmoid(mix_admit + bias_admit)
    log_decay = -decay_scale * keep_gate * jax.nn.softplus(-lambda_row)
    decays = jnp.exp(log_decay)
    injects = jnp.sqrt(-jnp.expm1(2.0 * log_decay)) * admit_gate * conv_out
    return (decays, injects)


def mlp_act(gate_in, upward_in):
    return jax.nn.gelu(gate_in) * upward_in


def combine_pairs(earlier, later):
    return (earlier[0] * later[0], later[0] * earlier[1] + later[1])


def matrix_shapes():
    return ((D, R), (D, R), (R, D), (D, F), (D, F), (F, D))


def split_tiles(tiles):
    matrices = []
    offset = 0
    for row_count, col_count in matrix_shapes():
        tile_count = row_count // TI * (col_count // TO)
        tile_block = tiles[offset : offset + tile_count].reshape(
            row_count // TI, col_count // TO, TI, TO
        )
        matrices.append(tile_block.transpose(0, 2, 1, 3).reshape(row_count, col_count))
        offset = offset + tile_count
    return tuple(matrices)


def join_tiles(matrices):
    pieces = []
    for matrix in matrices:
        row_count, col_count = matrix.shape
        pieces.append(
            matrix.reshape(row_count // TI, TI, col_count // TO, TO)
            .transpose(0, 2, 1, 3)
            .reshape(-1, TI, TO)
        )
    return jnp.concatenate(pieces, axis=0)


def carry_forward(decay_total, state_total):
    incoming = entering(
        (decay_total, state_total),
        "seq",
        combine_pairs,
        (jnp.ones_like(decay_total), jnp.zeros_like(state_total)),
        False,
    )
    return incoming[1]


def carry_backward(decay_total, grad_total):
    incoming = entering(
        (decay_total, grad_total),
        "seq",
        combine_pairs,
        (jnp.ones_like(decay_total), jnp.zeros_like(grad_total)),
        True,
    )
    return incoming[1]


def cholesky_qr(product):
    gram = jnp.einsum("nij,nik->njk", product, product, precision=highest)
    factor = jnp.linalg.cholesky(gram)
    return lax.linalg.triangular_solve(
        factor, product, left_side=False, lower=True, transpose_a=True
    )


def soap_update(grads, first, second, weight, basis_l, basis_r, stat_l, stat_r):
    rotated = jnp.einsum("nij,nik,nkl->njl", basis_l, grads, basis_r, precision=highest)
    first_new = beta_one * first + (1.0 - beta_one) * rotated
    second_new = beta_two * second + (1.0 - beta_two) * rotated * rotated
    direction = (
        first_new
        / (1.0 - beta_one**STEPNUM)
        / (jnp.sqrt(second_new / (1.0 - beta_two**STEPNUM)) + adam_eps)
    )
    update = jnp.einsum("nij,njk,nlk->nil", basis_l, direction, basis_r, precision=highest)
    weight_new = weight - learn_rate * (update + decay_rate * weight)
    stat_l_new = beta_two * stat_l + (1.0 - beta_two) * jnp.einsum(
        "nij,nkj->nik", grads, grads, precision=highest
    )
    stat_r_new = beta_two * stat_r + (1.0 - beta_two) * jnp.einsum(
        "nji,njk->nik", grads, grads, precision=highest
    )
    basis_l_new = cholesky_qr(jnp.einsum("nij,njk->nik", stat_l_new, basis_l, precision=highest))
    basis_r_new = cholesky_qr(jnp.einsum("nij,njk->nik", stat_r_new, basis_r, precision=highest))
    return (first_new, second_new, weight_new, basis_l_new, basis_r_new, stat_l_new, stat_r_new)


def adam_update(grads, first, second, weight, rate):
    first_new = beta_one * first + (1.0 - beta_one) * grads
    second_new = beta_two * second + (1.0 - beta_two) * grads * grads
    direction = (
        first_new
        / (1.0 - beta_one**STEPNUM)
        / (jnp.sqrt(second_new / (1.0 - beta_two**STEPNUM)) + adam_eps)
    )
    return (first_new, second_new, weight - rate * direction)


def on_device(
    block_input,
    cotangent,
    lengths,
    norm_gains,
    chan_params,
    gate_blocks,
    gains_first,
    gains_second,
    chan_first,
    chan_second,
    gate_first,
    gate_second,
    tile_weights,
    tile_first,
    tile_second,
    basis_left,
    basis_right,
    stat_left,
    stat_right,
    tile_of_slot,
):
    tokens = block_input[0]
    token_count = tokens.shape[0]
    place_index = lax.axis_index("seq")
    positions = place_index * token_count + jnp.arange(token_count, dtype=jnp.int32)
    valid_mask = (positions < lengths[0]).astype(jnp.float32)[:, None]
    gathered = lax.all_gather(tile_weights.astype(jnp.bfloat16), ("seq", "bat"), axis=0, tiled=True)
    tile_total = gathered.shape[0]
    inverse = (
        jnp.zeros((tile_total,), jnp.int32)
        .at[tile_of_slot]
        .set(jnp.arange(tile_total, dtype=jnp.int32))
    )
    input_weight, branch_weight, output_weight, gate_weight, upward_weight, down_weight = (
        split_tiles(jnp.take(gathered, inverse, axis=0))
    )
    gates_low = gate_blocks.astype(jnp.bfloat16)
    first_gain = norm_gains[0]
    second_gain = norm_gains[1]
    hidden_one = rms_norm(tokens, first_gain).astype(jnp.bfloat16)
    conv_in = multiply(hidden_one, input_weight)
    branch_pre = multiply(hidden_one, branch_weight)
    branch, branch_back = jax.vjp(jax.nn.gelu, branch_pre)
    edge_rows = passed_along(conv_in[token_count - (CONV - 1) :], "seq", 1)
    padded_in = jnp.concatenate([edge_rows, conv_in], axis=0)
    conv_sum = chan_params[CONV] + jnp.zeros_like(conv_in)
    for tap_index in range(CONV):
        conv_sum = (
            conv_sum
            + chan_params[tap_index]
            * padded_in[CONV - 1 - tap_index : CONV - 1 - tap_index + token_count]
        )
    conv_low = conv_sum.astype(jnp.bfloat16)
    conv_out = conv_low.astype(jnp.float32)
    mix_keep = block_apply(conv_low, gates_low[0])
    mix_admit = block_apply(conv_low, gates_low[1])
    (decays, injects), piece_back = jax.vjp(
        gate_piece,
        mix_keep,
        mix_admit,
        conv_out,
        chan_params[CONV + 1],
        chan_params[CONV + 2],
        chan_params[CONV + 3],
    )
    cum_decay, local_state = lax.associative_scan(combine_pairs, (decays, injects), axis=0)
    state_in = carry_forward(cum_decay[-1], local_state[-1])
    states = local_state + cum_decay * state_in
    mixed_low = (states * branch).astype(jnp.bfloat16)
    residual_mid = tokens + multiply(mixed_low, output_weight)
    hidden_two = rms_norm(residual_mid, second_gain).astype(jnp.bfloat16)
    gate_pre = multiply(hidden_two, gate_weight)
    upward_pre = multiply(hidden_two, upward_weight)
    mlp_value, mlp_back = jax.vjp(mlp_act, gate_pre, upward_pre)
    mlp_low = mlp_value.astype(jnp.bfloat16)
    block_output = residual_mid + multiply(mlp_low, down_weight)
    masked_grad = cotangent[0] * valid_mask
    masked_low = masked_grad.astype(jnp.bfloat16)
    down_weight_grad = contract_rows(mlp_low, masked_low)
    grad_mlp = multiply_transposed(masked_low, down_weight)
    grad_gate_pre, grad_upward_pre = mlp_back(grad_mlp)
    gate_grad_low = grad_gate_pre.astype(jnp.bfloat16)
    upward_grad_low = grad_upward_pre.astype(jnp.bfloat16)
    gate_weight_grad = contract_rows(hidden_two, gate_grad_low)
    upward_weight_grad = contract_rows(hidden_two, upward_grad_low)
    grad_hidden_two = multiply_transposed(gate_grad_low, gate_weight) + multiply_transposed(
        upward_grad_low, upward_weight
    )
    norm_two_out, norm_two_back = jax.vjp(rms_norm, residual_mid, second_gain)
    grad_mid_norm, second_gain_grad = norm_two_back(grad_hidden_two)
    grad_mid = masked_grad + grad_mid_norm
    mid_low = grad_mid.astype(jnp.bfloat16)
    output_weight_grad = contract_rows(mixed_low, mid_low)
    grad_mixed = multiply_transposed(mid_low, output_weight)
    branch_grad_low = branch_back(grad_mixed * states)[0].astype(jnp.bfloat16)
    next_decay = jnp.concatenate([decays[1:], jnp.ones_like(decays[:1])], axis=0)
    tail_decay, local_grad = lax.associative_scan(
        combine_pairs, (next_decay, grad_mixed * branch), axis=0, reverse=True
    )
    grad_in = carry_backward(decays[0] * tail_decay[0], decays[0] * local_grad[0])
    state_grad = local_grad + tail_decay * grad_in
    previous_states = jnp.concatenate([state_in[None], states[:-1]], axis=0)
    grad_keep, grad_admit, grad_conv_direct, grad_bias_keep, grad_bias_admit, grad_lambda = (
        piece_back((state_grad * previous_states, state_grad))
    )
    keep_low = grad_keep.astype(jnp.bfloat16)
    admit_low = grad_admit.astype(jnp.bfloat16)
    gate_blocks_grad = jnp.stack(
        [block_weight_grad(conv_low, keep_low), block_weight_grad(conv_low, admit_low)]
    )
    conv_grad = (
        grad_conv_direct + block_back(keep_low, gates_low[0]) + block_back(admit_low, gates_low[1])
    )
    edge_grads = passed_along(conv_grad[: CONV - 1], "seq", -1)
    extended = jnp.concatenate([conv_grad, edge_grads], axis=0)
    conv_in_grad = jnp.zeros_like(conv_grad)
    tap_grads = []
    for tap_index in range(CONV):
        conv_in_grad = (
            conv_in_grad + chan_params[tap_index] * extended[tap_index : tap_index + token_count]
        )
        tap_grads.append(
            jnp.sum(
                conv_grad * padded_in[CONV - 1 - tap_index : CONV - 1 - tap_index + token_count],
                axis=0,
            )
        )
    conv_bias_grad = jnp.sum(conv_grad, axis=0)
    conv_in_low = conv_in_grad.astype(jnp.bfloat16)
    input_weight_grad = contract_rows(hidden_one, conv_in_low)
    branch_weight_grad = contract_rows(hidden_one, branch_grad_low)
    grad_hidden_one = multiply_transposed(conv_in_low, input_weight) + multiply_transposed(
        branch_grad_low, branch_weight
    )
    norm_one_out, norm_one_back = jax.vjp(rms_norm, tokens, first_gain)
    grad_tokens_norm, first_gain_grad = norm_one_back(grad_hidden_one)
    input_grad = grad_mid + grad_tokens_norm
    small_terms = (
        jnp.stack([first_gain_grad, second_gain_grad]),
        jnp.stack(tap_grads + [conv_bias_grad, grad_bias_keep, grad_bias_admit, grad_lambda]),
        gate_blocks_grad,
    )
    gains_grad, chan_grad, gates_grad = lax.psum(
        (small_terms[0], small_terms[1], small_terms[2]), ("seq", "bat")
    )
    slot_grads = jnp.take(
        join_tiles(
            (
                input_weight_grad,
                branch_weight_grad,
                output_weight_grad,
                gate_weight_grad,
                upward_weight_grad,
                down_weight_grad,
            )
        ),
        tile_of_slot,
        axis=0,
    )
    own_grads = lax.psum_scatter(slot_grads, ("seq", "bat"), scatter_dimension=0, tiled=True)
    soap_out = soap_update(
        own_grads,
        tile_first,
        tile_second,
        tile_weights,
        basis_left,
        basis_right,
        stat_left,
        stat_right,
    )
    gains_out = adam_update(gains_grad, gains_first, gains_second, norm_gains, small_rate)
    chan_out = adam_update(chan_grad, chan_first, chan_second, chan_params, small_rate)
    gate_out = adam_update(gates_grad, gate_first, gate_second, gate_blocks, learn_rate)
    return (
        block_output[None],
        input_grad[None],
        gains_out[0],
        gains_out[1],
        gains_out[2],
        chan_out[0],
        chan_out[1],
        chan_out[2],
        gate_out[0],
        gate_out[1],
        gate_out[2],
        soap_out[0],
        soap_out[1],
        soap_out[2],
        soap_out[3],
        soap_out[4],
        soap_out[5],
        soap_out[6],
    )


def solution(mesh):
    return jax.shard_map(
        on_device,
        mesh=mesh,
        in_specs=(
            P("bat", "seq", None),
            P("bat", "seq", None),
            P("bat"),
            P(),
            P(),
            P(),
            P(),
            P(),
            P(),
            P(),
            P(),
            P(),
            P(("seq", "bat"), None, None),
            P(("seq", "bat"), None, None),
            P(("seq", "bat"), None, None),
            P(("seq", "bat"), None, None),
            P(("seq", "bat"), None, None),
            P(("seq", "bat"), None, None),
            P(("seq", "bat"), None, None),
            P(),
        ),
        out_specs=(
            P("bat", "seq", None),
            P("bat", "seq", None),
            P(),
            P(),
            P(),
            P(),
            P(),
            P(),
            P(),
            P(),
            P(),
            P(("seq", "bat"), None, None),
            P(("seq", "bat"), None, None),
            P(("seq", "bat"), None, None),
            P(("seq", "bat"), None, None),
            P(("seq", "bat"), None, None),
            P(("seq", "bat"), None, None),
            P(("seq", "bat"), None, None),
        ),
        check_vma=False,
    )
```

profile of v0, /device:TPU:0, one launch (start us, length us, event | category | flops | bytes accessed | tf_op | source)
XLA Modules:
  0.0 4714.7 jit_solution(16137718271773629996)
XLA Ops:
  13.8 17.0 scatter_custom_fusion
  33.2 150.9 %all-gather.6.cloned.1.call-done = bf16[3456,32,128]{2,1,0:T(8,128)(2,1)} async-done(((bf16[108,32,128]{2,1,0:T(8,128)(2,1)}), bf16[3456,32,128]{2,1,0:T(8,128)(2,1)}) %all-gather.6.cloned.1.call-update) | async-done | bytes 28311568 | tf_op jit(solution)/shard_map/all_gather | solution.py:230
  184.1 22.0 gather_fusion
  206.1 19.3 broadcast_select_fusion.1
  667.4 13.5 fusion.9
  715.7 12.7 slice.787
  728.4 12.9 slice.780
  741.3 12.8 slice.784
  754.1 13.3 slice.782
  893.9 13.1 slice.778
  907.0 13.2 slice.848
  1066.3 24.5 rev.8
  1090.9 24.7 rev.9
  1192.5 12.2 multiply_reduce_fusion.1
  1244.3 12.3 copy.202
  1256.6 11.5 copy.165
  1268.1 12.2 copy.203
  1280.3 11.8 copy.166
  1319.1 11.2 constant_dynamic-update-slice_fusion.2
  1352.0 41.0 gather_fusion.1
  1393.0 38.1 broadcast_select_fusion
  1439.5 17.4 add_bitcast_fusion
  1456.9 40.9 all-reduce.74
  1507.6 396.9 %reduce-scatter.2.cloned.1.call-done = f32[108,32,128]{2,1,0:T(8,128)} async-done(((f32[3456,32,128]{2,1,0:T(8,128)}), f32[108,32,128]{2,1,0:T(8,128)}) %reduce-scatter.2.cloned.1.call-update) | async-done | bytes 1769488 | tf_op jit(solution)/shard_map/reduce_scatter | solution.py:363
  1933.7 12.7 multiply_subtract_fusion.1
  1951.9 317.0 %custom-call.14 = f32[108,32,32]{2,1,0:T(8,128)S(1)} custom-call(f32[108,32,32]{2,1,0:T(8,128)} %fusion.86), custom_call_target="Cholesky" | custom-call | tf_op jit(solution)/shard_map/jit(cholesky)/cholesky | solution.py:164
  2271.8 12.6 custom-call.15
  2296.5 14.4 multiply_add_fusion.2
  2323.3 14.5 fusion.191
  2356.7 1267.9 %custom-call.16 = f32[108,128,128]{2,1,0:T(8,128)} custom-call(f32[108,128,128]{2,1,0:T(8,128)} %fusion.2), custom_call_target="Cholesky" | custom-call | tf_op jit(solution)/shard_map/jit(cholesky)/cholesky | solution.py:164
  3633.4 1062.3 %custom-call.17 = f32[108,1,128,128]{2,3,1,0:T(8,128)} custom-call(f32[108,1,128,128]{3,2,1,0:T(8,128)} %select_bitcast_fusion), custom_call_target="InvertDiagBlocksLowerTriangular" | custom-call | tf_op jit(solution)/shard_map/triangular_solve | solution.py:165
  4695.7 12.3 fusion
  (784 shorter events, 1028.6 us)
Async XLA Ops:
  7.2 176.9 %all-gather.6.cloned.1.call-start = ((), (), s32[]{:S(2)}) async-start(), calls=%async_computation.1 | async-start | bytes 29196288 | tf_op jit(solution)/shard_map/all_gather | solution.py:230
  9.8 1489.3 %all-reduce.77.cloned.1.call-start = ((), (), s32[]{:S(2)}) async-start(), calls=%async_computation.2 | async-start | bytes 6291456 | tf_op jit(solution)/shard_map/psum | solution.py:346
  30.9 227.1 %copy-start.152 = (f32[512]{0:T(512)}, f32[512]{0:T(512)S(1)}, u32[]{:S(2)}) copy-start(f32[512]{0:T(512)S(1)} %fusion.150) | copy-start | bytes 6148
  31.7 174.4 %copy-start.146 = (f32[512]{0:T(512)}, f32[512]{0:T(512)S(1)}, u32[]{:S(2)}) copy-start(f32[512]{0:T(512)S(1)} %fusion.82) | copy-start | bytes 6148
  31.8 209.7 %copy-start.148 = (f32[512]{0:T(512)}, f32[512]{0:T(512)S(1)}, u32[]{:S(2)}) copy-start(f32[512]{0:T(512)S(1)} %fusion.151) | copy-start | bytes 6148
  31.8 209.7 %copy-start.111 = (f32[1,1024]{1,0:T(1,128)}, f32[1,1024]{1,0:T(1,128)S(1)}, u32[]{:S(2)}) copy-start(f32[1,1024]{1,0:T(1,128)S(1)} %get-tuple-element.381) | copy-start | bytes 12292
  32.5 173.7 %copy-start.87 = (f32[1536]{0:T(1024)}, f32[1536]{0:T(1024)S(1)}, u32[]{:S(2)}) copy-start(f32[1536]{0:T(1024)S(1)} %get-tuple-element.350) | copy-start | bytes 18436
  32.5 253.2 %copy-start.95 = (f32[1536]{0:T(1024)}, f32[1536]{0:T(1024)S(1)}, u32[]{:S(2)}) copy-start(f32[1536]{0:T(1024)S(1)} %get-tuple-element.233) | copy-start | bytes 18436
  32.5 253.2 %copy-start.97 = (f32[1536]{0:T(1024)}, f32[1536]{0:T(1024)S(1)}, u32[]{:S(2)}) copy-start(f32[1536]{0:T(1024)S(1)} %get-tuple-element.234) | copy-start | bytes 18436
  32.5 253.3 %copy-start.99 = (f32[1536]{0:T(1024)}, f32[1536]{0:T(1024)S(1)}, u32[]{:S(2)}) copy-start(f32[1536]{0:T(1024)S(1)} %get-tuple-element.235) | copy-start | bytes 18436
  32.5 253.3 %copy-start.101 = (f32[1536]{0:T(1024)}, f32[1536]{0:T(1024)S(1)}, u32[]{:S(2)}) copy-start(f32[1536]{0:T(1024)S(1)} %get-tuple-element.236) | copy-start | bytes 18436
  32.5 268.4 %copy-start.75 = (f32[1536]{0:T(1024)}, f32[1536]{0:T(1024)S(1)}, u32[]{:S(2)}) copy-start(f32[1536]{0:T(1024)S(1)} %get-tuple-element.232) | copy-start | bytes 18436
  32.5 268.4 %copy-start.81 = (f32[1536]{0:T(1024)}, f32[1536]{0:T(1024)S(1)}, u32[]{:S(2)}) copy-start(f32[1536]{0:T(1024)S(1)} %get-tuple-element.231) | copy-start | bytes 18436
  32.6 268.4 %copy-start.79 = (f32[1536]{0:T(1024)}, f32[1536]{0:T(1024)S(1)}, u32[]{:S(2)}) copy-start(f32[1536]{0:T(1024)S(1)} %broadcast_multiply_fusion) | copy-start | bytes 18436
  245.1 40.6 collective-permute-start
  656.1 37.6 copy-start.36
  658.1 34.0 copy-start.37
  893.9 30.8 copy-start.85
  1090.9 40.6 copy-start.2
  1090.9 40.6 copy-start.76
  1090.9 40.6 copy-start.80
  1090.9 40.6 copy-start.82
  1206.4 85.8 %collective-permute-start.1 = (f32[3,1536]{1,0:T(4,128)S(1)}, f32[3,1536]{1,0:T(4,128)S(1)}, u32[]{:S(2)}, u32[]{:S(2)}) collective-permute-start(f32[3,1536]{1,0:T(4,128)S(1)} %slice.1006), channel_id=1, source_target_pairs={{8,0},{16,8},{24,16},{9,1},{17,9},{25,17},{10,2},{18,10},{26,18},{... | collective-permute-start | bytes 55304 | tf_op jit(solution)/shard_map/ppermute | solution.py:47
  1209.6 695.0 %reduce-scatter.2.cloned.1.call-start = ((), (), s32[]{:S(2)}) async-start(), calls=%async_computation.3 | async-start | bytes 58392576 | tf_op jit(solution)/shard_map/reduce_scatter | solution.py:363
  1352.0 41.0 copy-start.151
  1439.4 58.4 %copy-start.123 = (f32[2,1024]{1,0:T(2,128)S(1)}, f32[2,1024]{1,0:T(2,128)}, u32[]{:S(2)}) copy-start(f32[2,1024]{1,0:T(2,128)} %param.27) | copy-start | bytes 24580
  1439.4 58.4 %copy-start.154 = (f32[2,1024]{1,0:T(2,128)S(1)}, f32[2,1024]{1,0:T(2,128)}, u32[]{:S(2)}) copy-start(f32[2,1024]{1,0:T(2,128)} %param.31) | copy-start | bytes 24580
  1439.4 58.4 %copy-start.155 = (f32[2,1024]{1,0:T(2,128)S(1)}, f32[2,1024]{1,0:T(2,128)}, u32[]{:S(2)}) copy-start(f32[2,1024]{1,0:T(2,128)} %param.30) | copy-start | bytes 24580
  1439.4 59.1 %copy-start.109 = (f32[8,1536]{1,0:T(8,128)S(1)}, f32[8,1536]{1,0:T(8,128)}, u32[]{:S(2)}) copy-start(f32[8,1536]{1,0:T(8,128)} %param.33) | copy-start | bytes 147460
  1439.4 59.1 %copy-start.110 = (f32[8,1536]{1,0:T(8,128)S(1)}, f32[8,1536]{1,0:T(8,128)}, u32[]{:S(2)}) copy-start(f32[8,1536]{1,0:T(8,128)} %param.32) | copy-start | bytes 147460
  1439.4 59.7 %copy-start.35 = (f32[2,8,192,192]{3,2,1,0:T(8,128)S(1)}, f32[2,8,192,192]{3,2,1,0:T(8,128)}, u32[]{:S(2)}) copy-start(f32[2,8,192,192]{3,2,1,0:T(8,128)} %param.29) | copy-start | bytes 7077892
  2346.3 1278.2 %copy-start.103 = (pred[128,128]{1,0:T(8,128)(4,1)S(1)}, pred[128,128]{1,0:T(8,128)(4,1)}, u32[]{:S(2)}) copy-start(pred[128,128]{1,0:T(8,128)(4,1)} %iota_compare_fusion) | copy-start | bytes 49156
  (144 other events, 1298.4 us)
Sparse Core Ops, SparseCore 0:
  11.6 172.4 all-gather.5
  1209.7 137.7 all-reduce.76
  1431.2 473.2 reduce-scatter.1
where the time goes:
time: 4740 us; the launch traced here: 4710 us
  other arithmetic  2960 us (62%)
  local copies, waits for them, and re-layouts  881 us (19%)
  waiting for transfers between devices  548 us (12%)
  matrix products  235 us (5%)
  blocking collectives  71.8 us (2%)
    another operation x8, other arithmetic, cholesky_qr(): factor = jnp.linalg.cholesky(gram)  1590 us
    another operation x6, other arithmetic, cholesky_qr(): lax.linalg.triangular_solve(factor, product, left_side=False, lower=True,...  1080 us
    reduce_scatter x1, waiting for transfers between devices, on_device(): lax.psum_scatter(slot_grads, ('seq', 'bat'), scatter_dimension=0, tiled=T...  397 us
    slice x65, local copies, waits for them, and re-layouts, on_device(): lax.associative_scan(combine_pairs, (next_decay, grad_mixed * branch), ax...  219 us
    all_gather x1, waiting for transfers between devices, on_device(): lax.all_gather(tile_weights.astype(jnp.bfloat16), ('seq', 'bat'), axis=0,...  151 us
    slice x60, local copies, waits for them, and re-layouts, on_device(): lax.associative_scan(combine_pairs, (decays, injects), axis=0)  134 us
    unnamed x359, local copies, waits for them, and re-layouts  95.2 us
  transfers between devices with their start and end apart: 5, of which 2 were waited for; matrix products, arithmetic and copies ran while one was open for 7% of the time, Pallas kernels for 0%

commit v1 on v0

--- a/solution.py
+++ b/solution.py
@@ -1,6 +1,10 @@
+import functools
+
 import jax
 import jax.numpy as jnp
 from jax import lax
+from jax.experimental import pallas as pl
+from jax.experimental.pallas import tpu as pltpu
 from jax.sharding import PartitionSpec as P
 
 D = 1024
@@ -12,6 +16,11 @@
 TO = 128
 STEPNUM = 10
 BS = 192
+GC = 384
+LANES = GC // 128
+SEG = 8
+f32 = jnp.float32
+bf16 = jnp.bfloat16
 
 
 highest = lax.Precision.HIGHEST
@@ -25,20 +34,16 @@
 decay_scale = 8.0
 
 
-def entering(part, axis, combine, identity, reverse):
+def entering(factor, total, axis, reverse):
     count = lax.axis_size(axis)
     place = lax.axis_index(axis)
-    ahead = count - 1 - place if reverse else place
-    gathered = jax.tree.map(lambda a: lax.all_gather(a, axis), part)
-    state = jax.tree.map(lambda a, e: jnp.zeros_like(a) + jnp.asarray(e, a.dtype), part, identity)
-
-    def one(step, state):
+    gathered = lax.all_gather(jnp.stack([factor, total]), axis)
+    state = jnp.zeros_like(total)
+    for step in range(count):
         source = count - 1 - step if reverse else step
-        return combine(
-            state, jax.tree.map(lambda a: lax.dynamic_index_in_dim(a, source, 0, False), gathered)
-        )
-
-    return lax.fori_loop(0, ahead, one, state)
+        passed = source > place if reverse else source < place
+        state = jnp.where(passed, gathered[source, 1] + gathered[source, 0] * state, state)
+    return state
 
 
 def passed_along(value, axis, by):
@@ -65,47 +70,217 @@
     )
 
 
-def block_apply(values_low, blocks_low):
-    token_count = values_low.shape[0]
-    split_view = values_low.reshape(token_count, HB, BS)
-    return jnp.einsum(
-        "tbi,bij->tbj", split_view, blocks_low, preferred_element_type=jnp.float32
-    ).reshape(token_count, R)
-
-
-def block_back(grads_low, blocks_low):
-    token_count = grads_low.shape[0]
-    split_view = grads_low.reshape(token_count, HB, BS)
-    return jnp.einsum(
-        "tbj,bij->tbi", split_view, blocks_low, preferred_element_type=jnp.float32
-    ).reshape(token_count, R)
-
-
-def block_weight_grad(values_low, grads_low):
-    token_count = values_low.shape[0]
-    return jnp.einsum(
-        "tbi,tbj->bij",
-        values_low.reshape(token_count, HB, BS),
-        grads_low.reshape(token_count, HB, BS),
-        preferred_element_type=jnp.float32,
-    )
-
-
-def gate_piece(mix_keep, mix_admit, conv_out, bias_keep, bias_admit, lambda_row):
-    keep_gate = jax.nn.sigmoid(mix_keep + bias_keep)
-    admit_gate = jax.nn.sigmoid(mix_admit + bias_admit)
-    log_decay = -decay_scale * keep_gate * jax.nn.softplus(-lambda_row)
+def gate_values(conv_low, keep_block, admit_block, rows):
+    mix_keep = jnp.dot(conv_low, keep_block, preferred_element_type=f32)
+    mix_admit = jnp.dot(conv_low, admit_block, preferred_element_type=f32)
+    keep_gate = jax.nn.sigmoid(mix_keep + rows[CONV + 1 : CONV + 2])
+    admit_gate = jax.nn.sigmoid(mix_admit + rows[CONV + 2 : CONV + 3])
+    log_decay = (-decay_scale * rows[CONV + 3 : CONV + 4]) * keep_gate
     decays = jnp.exp(log_decay)
-    injects = jnp.sqrt(-jnp.expm1(2.0 * log_decay)) * admit_gate * conv_out
-    return (decays, injects)
+    twice = 2.0 * log_decay
+    series = 1.0 + twice * (1.0 / 7.0)
+    for order in (6.0, 5.0, 4.0, 3.0, 2.0):
+        series = 1.0 + twice * (1.0 / order) * series
+    drop = jnp.where(twice > -0.4, -twice * series, 1.0 - decays * decays)
+    return keep_gate, admit_gate, decays, drop
+
+def forward_kernel(conv_in_ref, edge_ref, rows_ref, keep_ref, admit_ref,
+                   conv_low_ref, decays_ref, prod_ref, local_ref, padded, factors, terms):
+    tokens = conv_in_ref.shape[0]
+    rows = rows_ref[...]
+    padded[0:8, :] = edge_ref[...]
+    padded[pl.ds(8, tokens), :] = conv_in_ref[...]
+    conv = rows[CONV : CONV + 1] + rows[0:1] * conv_in_ref[...]
+    for tap in range(1, CONV):
+        conv += rows[tap : tap + 1] * padded[pl.ds(8 - tap, tokens), :]
+    conv_low = conv.astype(bf16)
+    conv_low_ref[...] = conv_low
+    keep_gate, admit_gate, decays, drop = gate_values(conv_low, keep_ref[0], admit_ref[0], rows)
+    decays_ref[...] = decays
+    injects = jnp.sqrt(drop) * admit_gate * conv_low.astype(f32)
+    for part in range(LANES):
+        factors[pl.ds(part * tokens, tokens), :] = decays[:, part * 128 : part * 128 + 128]
+        terms[pl.ds(part * tokens, tokens), :] = injects[:, part * 128 : part * 128 + 128]
+    length = tokens // SEG
+
+    def one(t, carry):
+        result = []
+        for part in range(LANES):
+            prod, local = carry[part]
+            at = pl.ds(part * tokens + t, SEG, stride=length)
+            decay = factors[at, :]
+            prod = prod * decay
+            local = decay * local + terms[at, :]
+            factors[at, :] = prod
+            terms[at, :] = local
+            result.append((prod, local))
+        return tuple(result)
+
+    start = (jnp.ones((SEG, 128), f32), jnp.zeros((SEG, 128), f32))
+    lax.fori_loop(0, length, one, (start,) * LANES, unroll=8)
+    for part in range(LANES):
+        prod_ref[:, part * 128 : part * 128 + 128] = factors[pl.ds(part * tokens, tokens), :]
+        local_ref[:, part * 128 : part * 128 + 128] = terms[pl.ds(part * tokens, tokens), :]
+
+def col(block_rows):
+    return pl.BlockSpec((block_rows, GC), lambda g: (0, g))
+
+def mat():
+    return pl.BlockSpec((1, GC, GC), lambda g: (g, 0, 0))
+
+def recurrent_forward(conv_in, edge, rows, keep_blocks, admit_blocks):
+    tokens = conv_in.shape[0]
+    full = lambda dt: jax.ShapeDtypeStruct((tokens, R), dt)
+    return pl.pallas_call(
+        forward_kernel,
+        grid=(R // GC,),
+        out_shape=(full(bf16), full(f32), full(f32), full(f32)),
+        in_specs=[col(tokens), col(8), col(8), mat(), mat()],
+        out_specs=[col(tokens)] * 4,
+        scratch_shapes=[pltpu.VMEM((tokens + 8, GC), f32)] + [pltpu.VMEM((LANES * tokens, 128), f32)] * 2,
+        compiler_params=pltpu.CompilerParams(vmem_limit_bytes=48 * 2**20),
+        name="recurrence_forward",
+    )(conv_in, edge, rows, keep_blocks, admit_blocks)
+
+def reverse_kernel(decays_ref, source_ref, prod_ref, local_ref, padded, factors, terms):
+    tokens = decays_ref.shape[0]
+    length = tokens // SEG
+    padded[pl.ds(0, tokens), :] = decays_ref[...]
+    padded[pl.ds(tokens, 8), :] = jnp.ones((8, decays_ref.shape[1]), f32)
+    for part in range(LANES):
+        factors[pl.ds(part * tokens, tokens), :] = padded[pl.ds(1, tokens), part * 128 : part * 128 + 128]
+        terms[pl.ds(part * tokens, tokens), :] = source_ref[:, part * 128 : part * 128 + 128]
+
+    def one(step, carry):
+        result = []
+        for part in range(LANES):
+            prod, local = carry[part]
+            at = pl.ds(part * tokens + length - 1 - step, SEG, stride=length)
+            decay = factors[at, :]
+            prod = prod * decay
+            local = decay * local + terms[at, :]
+            factors[at, :] = prod
+            terms[at, :] = local
+            result.append((prod, local))
+        return tuple(result)
+
+    start = (jnp.ones((SEG, 128), f32), jnp.zeros((SEG, 128), f32))
+    lax.fori_loop(0, length, one, (start,) * LANES, unroll=8)
+    for part in range(LANES):
+        prod_ref[:, part * 128 : part * 128 + 128] = factors[pl.ds(part * tokens, tokens), :]
+        local_ref[:, part * 128 : part * 128 + 128] = terms[pl.ds(part * tokens, tokens), :]
+
+def recurrent_reverse(decays, source):
+    tokens = decays.shape[0]
+    full = jax.ShapeDtypeStruct((tokens, R), f32)
+    return pl.pallas_call(
+        reverse_kernel,
+        grid=(R // GC,),
+        out_shape=(full, full),
+        in_specs=[col(tokens)] * 2,
+        out_specs=[col(tokens)] * 2,
+        scratch_shapes=[pltpu.VMEM((tokens + 8, GC), f32)] + [pltpu.VMEM((LANES * tokens, 128), f32)] * 2,
+        compiler_params=pltpu.CompilerParams(vmem_limit_bytes=48 * 2**20),
+        name="recurrence_reverse",
+    )(decays, source)
+
+def spread(carry, tokens):
+    length = tokens // SEG
+    return jnp.concatenate(
+        [jnp.broadcast_to(carry[s : s + 1], (length, carry.shape[1])) for s in range(SEG)], axis=0)
+
+def gate_back_kernel(conv_low_ref, states_ref, before_ref, prod_ref, local_ref, carry_ref, rows_ref,
+                     keep_ref, admit_ref, conv_grad_ref, keep_grad_ref, admit_grad_ref, sums_ref, padded):
+    tokens = conv_low_ref.shape[0]
+    rows = rows_ref[...]
+    conv_low = conv_low_ref[...]
+    conv_out = conv_low.astype(f32)
+    keep_gate, admit_gate, decays, drop = gate_values(conv_low, keep_ref[0], admit_ref[0], rows)
+    padded[0:8, :] = before_ref[...]
+    padded[pl.ds(8, tokens), :] = states_ref[...]
+    state_grad = local_ref[...] + prod_ref[...] * spread(carry_ref[...], tokens)
+    decay_grad = state_grad * padded[pl.ds(7, tokens), :]
+    root = jnp.sqrt(drop)
+    scaled = state_grad * conv_out
+    root_grad = scaled * admit_gate
+    log_grad = decay_grad * decays - root_grad * (decays * decays) / root
+    keep_grad = log_grad * (-decay_scale * rows[CONV + 3 : CONV + 4]) * (keep_gate * (1.0 - keep_gate))
+    admit_grad = scaled * root * (admit_gate * (1.0 - admit_gate))
+    sums_ref[0:1, :] = jnp.sum(keep_grad, axis=0, keepdims=True)
+    sums_ref[1:2, :] = jnp.sum(admit_grad, axis=0, keepdims=True)
+    sums_ref[2:3, :] = jnp.sum(log_grad * keep_gate, axis=0, keepdims=True) * -decay_scale
+    sums_ref[3:8, :] = jnp.zeros((5, rows.shape[1]), f32)
+    keep_low = keep_grad.astype(bf16)
+    admit_low = admit_grad.astype(bf16)
+    back = (((1,), (1,)), ((), ()))
+    over = (((0,), (0,)), ((), ()))
+    conv_grad_ref[...] = (
+        state_grad * root * admit_gate
+        + lax.dot_general(keep_low, keep_ref[0], back, preferred_element_type=f32)
+        + lax.dot_general(admit_low, admit_ref[0], back, preferred_element_type=f32)
+    )
+    keep_grad_ref[0] = lax.dot_general(conv_low, keep_low, over, preferred_element_type=f32)
+    admit_grad_ref[0] = lax.dot_general(conv_low, admit_low, over, preferred_element_type=f32)
+
+def gates_backward(conv_low, states, before, prod, local, carry, rows, keep_blocks, admit_blocks):
+    tokens = conv_low.shape[0]
+    blocks = jax.ShapeDtypeStruct((R // GC, GC, GC), f32)
+    return pl.pallas_call(
+        gate_back_kernel,
+        grid=(R // GC,),
+        out_shape=(jax.ShapeDtypeStruct((tokens, R), f32), blocks, blocks, jax.ShapeDtypeStruct((8, R), f32)),
+        in_specs=[col(tokens), col(tokens), col(8), col(tokens), col(tokens), col(8), col(8), mat(), mat()],
+        out_specs=[col(tokens), mat(), mat(), col(8)],
+        scratch_shapes=[pltpu.VMEM((tokens + 8, GC), f32)],
+        compiler_params=pltpu.CompilerParams(vmem_limit_bytes=56 * 2**20),
+        name="gates_backward",
+    )(conv_low, states, before, prod, local, carry, rows, keep_blocks, admit_blocks)
+
+def conv_back_kernel(conv_grad_ref, after_ref, conv_in_ref, before_ref, rows_ref, low_ref, sums_ref, ahead, behind):
+    tokens = conv_grad_ref.shape[0]
+    rows = rows_ref[...]
+    grads = conv_grad_ref[...]
+    ahead[pl.ds(0, tokens), :] = grads
+    ahead[pl.ds(tokens, 8), :] = after_ref[...]
+    behind[0:8, :] = before_ref[...]
+    behind[pl.ds(8, tokens), :] = conv_in_ref[...]
+    total = rows[0:1] * grads
+    sums_ref[0:1, :] = jnp.sum(grads * conv_in_ref[...], axis=0, keepdims=True)
+    for tap in range(1, CONV):
+        total += rows[tap : tap + 1] * ahead[pl.ds(tap, tokens), :]
+        sums_ref[tap : tap + 1, :] = jnp.sum(grads * behind[pl.ds(8 - tap, tokens), :], axis=0, keepdims=True)
+    sums_ref[CONV : CONV + 1, :] = jnp.sum(grads, axis=0, keepdims=True)
+    sums_ref[CONV + 1 : 8, :] = jnp.zeros((7 - CONV, rows.shape[1]), f32)
+    low_ref[...] = total.astype(bf16)
+
+def conv_backward(conv_grad, after, conv_in, before, rows):
+    tokens = conv_grad.shape[0]
+    return pl.pallas_call(
+        conv_back_kernel,
+        grid=(R // GC,),
+        out_shape=(jax.ShapeDtypeStruct((tokens, R), bf16), jax.ShapeDtypeStruct((8, R), f32)),
+        in_specs=[col(tokens), col(8), col(tokens), col(8), col(8)],
+        out_specs=[col(tokens), col(8)],
+        scratch_shapes=[pltpu.VMEM((tokens + 8, GC), f32)] * 2,
+        compiler_params=pltpu.CompilerParams(vmem_limit_bytes=48 * 2**20),
+        name="conv_backward",
+    )(conv_grad, after, conv_in, before, rows)
+
+def pair_blocks(blocks):
+    per = GC // BS
+    grouped = blocks.reshape(HB // per, per, BS, BS)
+    zero = jnp.zeros((HB // per, BS, BS), blocks.dtype)
+    lines = [jnp.concatenate([grouped[:, i] if i == j else zero for j in range(per)], axis=2) for i in range(per)]
+    return jnp.concatenate(lines, axis=1)
+
+def unpair_blocks(paired):
+    per = GC // BS
+    parts = [paired[:, i * BS : (i + 1) * BS, i * BS : (i + 1) * BS] for i in range(per)]
+    return jnp.stack(parts, axis=1).reshape(HB, BS, BS)
 
 
 def mlp_act(gate_in, upward_in):
     return jax.nn.gelu(gate_in) * upward_in
-
-
-def combine_pairs(earlier, later):
-    return (earlier[0] * later[0], later[0] * earlier[1] + later[1])
 
 
 def matrix_shapes():
@@ -137,34 +312,86 @@
     return jnp.concatenate(pieces, axis=0)
 
 
-def carry_forward(decay_total, state_total):
-    incoming = entering(
-        (decay_total, state_total),
-        "seq",
-        combine_pairs,
-        (jnp.ones_like(decay_total), jnp.zeros_like(state_total)),
-        False,
-    )
-    return incoming[1]
-
-
-def carry_backward(decay_total, grad_total):
-    incoming = entering(
-        (decay_total, grad_total),
-        "seq",
-        combine_pairs,
-        (jnp.ones_like(decay_total), jnp.zeros_like(grad_total)),
-        True,
-    )
-    return incoming[1]
+def chol_kernel(n, count, g_ref, m_ref, q_ref, aug, mult, winv):
+    nb = n // 8
+    lanes = 128
+    padrows = lanes - count
+    sub = lax.broadcasted_iota(jnp.int32, (n, lanes), 0)
+    def load(i, c):
+        x = g_ref[pl.ds(i, count, stride=n), :]
+        if padrows:
+            x = jnp.concatenate([x, jnp.zeros((padrows, n), f32)], axis=0)
+        aug[i, 0:n, :] = x.T
+        aug[i, n:2*n, :] = jnp.where(sub == i, 1.0, 0.0)
+        return c
+    lax.fori_loop(0, n, load, 0)
+
+    def step(kb, c):
+        k0 = pl.multiple_of(kb * 8, 8)
+        for r in range(8):
+            d = aug[k0 + r, pl.ds(k0 + r, 1), :]
+            inv = jnp.broadcast_to(lax.rsqrt(d), (8, lanes))
+            ms = [jnp.broadcast_to(aug[k0 + r, pl.ds(k0 + r2, 1), :], (8, lanes)) * inv for r2 in range(r + 1, 8)]
+            def prow(j, c, r=r, inv=inv, ms=ms):
+                j0 = pl.multiple_of((kb + j) * 8, 8)
+                u = aug[k0 + r, pl.ds(j0, 8), :] * inv
+                aug[k0 + r, pl.ds(j0, 8), :] = u
+                for q, r2 in enumerate(range(r + 1, 8)):
+                    aug[k0 + r2, pl.ds(j0, 8), :] -= ms[q] * u
+                return c
+            lax.fori_loop(0, nb + 1, prow, 0, unroll=True)
+        def rows(ib, c):
+            i0 = pl.multiple_of(ib * 8, 8)
+            for r in range(8):
+                for a in range(8):
+                    mult[r * 8 + a] = jnp.broadcast_to(aug[k0 + r, pl.ds(i0 + a, 1), :], (8, lanes))
+            def cols(j, c):
+                j0 = pl.multiple_of(j * 8, 8)
+                us = [aug[k0 + r, pl.ds(j0, 8), :] for r in range(8)]
+                for a in range(8):
+                    t = aug[i0 + a, pl.ds(j0, 8), :]
+                    p0 = mult[a] * us[0]
+                    p1 = mult[8 + a] * us[1]
+                    for r in range(2, 8, 2):
+                        p0 += mult[r * 8 + a] * us[r]
+                        p1 += mult[r * 8 + 8 + a] * us[r + 1]
+                    aug[i0 + a, pl.ds(j0, 8), :] = t - (p0 + p1)
+                return c
+            lax.fori_loop(ib, nb + kb + 1, cols, 0)
+            return c
+        lax.fori_loop(kb + 1, nb, rows, 0)
+        return c
+    lax.fori_loop(0, nb, step, 0)
+
+    def store(i, c):
+        w = aug[i, n:2*n, :].T
+        winv[pl.ds(i, count, stride=n), :] = w[:count]
+        return c
+    lax.fori_loop(0, n, store, 0)
+
+    def apply(b, c):
+        rows = pl.ds(pl.multiple_of(b * n, n), n)
+        q_ref[rows, :] = lax.dot_general(m_ref[rows, :], winv[rows, :], (((1,), (1,)), ((), ())),
+            precision=lax.Precision.HIGHEST, preferred_element_type=f32)
+        return c
+    lax.fori_loop(0, count, apply, 0, unroll=4 if count % 4 == 0 else 1)
+
+def chol_qr(gram, m):
+    count, n, _ = gram.shape
+    out = pl.pallas_call(
+        functools.partial(chol_kernel, n, count),
+        out_shape=jax.ShapeDtypeStruct((count * n, n), f32),
+        in_specs=[pl.BlockSpec(memory_space=pltpu.VMEM)] * 2,
+        out_specs=pl.BlockSpec(memory_space=pltpu.VMEM),
+        scratch_shapes=[pltpu.VMEM((n, 2 * n, 128), f32), pltpu.VMEM((64, 8, 128), f32), pltpu.VMEM((count * n, n), f32)],
+        compiler_params=pltpu.CompilerParams(vmem_limit_bytes=60 * 2**20),
+    )(gram.reshape(count * n, n), m.reshape(count * n, n))
+    return out.reshape(count, n, n)
 
 
 def cholesky_qr(product):
     gram = jnp.einsum("nij,nik->njk", product, product, precision=highest)
-    factor = jnp.linalg.cholesky(gram)
-    return lax.linalg.triangular_solve(
-        factor, product, left_side=False, lower=True, transpose_a=True
-    )
+    return chol_qr(gram, product)
 
 
 def soap_update(grads, first, second, weight, basis_l, basis_r, stat_l, stat_r):
@@ -235,7 +462,7 @@
         .set(jnp.arange(tile_total, dtype=jnp.int32))
     )
     input_weight, branch_weight, output_weight, gate_weight, upward_weight, down_weight = (
-        split_tiles(jnp.take(gathered, inverse, axis=0))
+        split_tiles(jnp.take(gathered, inverse, axis=0, mode="clip"))
     )
     gates_low = gate_blocks.astype(jnp.bfloat16)
     first_gain = norm_gains[0]
@@ -244,31 +471,24 @@
     conv_in = multiply(hidden_one, input_weight)
     branch_pre = multiply(hidden_one, branch_weight)
     branch, branch_back = jax.vjp(jax.nn.gelu, branch_pre)
+    rows = jnp.concatenate([chan_params[: CONV + 3], jax.nn.softplus(-chan_params[CONV + 3 :])], axis=0)
+    keep_blocks, admit_blocks = pair_blocks(gates_low[0]), pair_blocks(gates_low[1])
     edge_rows = passed_along(conv_in[token_count - (CONV - 1) :], "seq", 1)
-    padded_in = jnp.concatenate([edge_rows, conv_in], axis=0)
-    conv_sum = chan_params[CONV] + jnp.zeros_like(conv_in)
-    for tap_index in range(CONV):
-        conv_sum = (
-            conv_sum
-            + chan_params[tap_index]
-            * padded_in[CONV - 1 - tap_index : CONV - 1 - tap_index + token_count]
-        )
-    conv_low = conv_sum.astype(jnp.bfloat16)
-    conv_out = conv_low.astype(jnp.float32)
-    mix_keep = block_apply(conv_low, gates_low[0])
-    mix_admit = block_apply(conv_low, gates_low[1])
-    (decays, injects), piece_back = jax.vjp(
-        gate_piece,
-        mix_keep,
-        mix_admit,
-        conv_out,
-        chan_params[CONV + 1],
-        chan_params[CONV + 2],
-        chan_params[CONV + 3],
-    )
-    cum_decay, local_state = lax.associative_scan(combine_pairs, (decays, injects), axis=0)
-    state_in = carry_forward(cum_decay[-1], local_state[-1])
-    states = local_state + cum_decay * state_in
+    edge_rows = jnp.pad(edge_rows, ((9 - CONV, 0), (0, 0)))
+    conv_low, decays, product, local_state = recurrent_forward(
+        conv_in, edge_rows, rows, keep_blocks, admit_blocks
+    )
+    length = token_count // SEG
+    factors = [product[(s + 1) * length - 1] for s in range(SEG)]
+    totals = [local_state[(s + 1) * length - 1] for s in range(SEG)]
+    factor, total = factors[0], totals[0]
+    for s in range(1, SEG):
+        factor, total = factor * factors[s], totals[s] + factors[s] * total
+    state_in = entering(factor, total, "seq", False)
+    carries = [state_in]
+    for s in range(SEG - 1):
+        carries.append(totals[s] + factors[s] * carries[-1])
+    states = local_state + product * spread(jnp.stack(carries), token_count)
     mixed_low = (states * branch).astype(jnp.bfloat16)
     residual_mid = tokens + multiply(mixed_low, output_weight)
     hidden_two = rms_norm(residual_mid, second_gain).astype(jnp.bfloat16)
@@ -296,40 +516,26 @@
     output_weight_grad = contract_rows(mixed_low, mid_low)
     grad_mixed = multiply_transposed(mid_low, output_weight)
     branch_grad_low = branch_back(grad_mixed * states)[0].astype(jnp.bfloat16)
-    next_decay = jnp.concatenate([decays[1:], jnp.ones_like(decays[:1])], axis=0)
-    tail_decay, local_grad = lax.associative_scan(
-        combine_pairs, (next_decay, grad_mixed * branch), axis=0, reverse=True
-    )
-    grad_in = carry_backward(decays[0] * tail_decay[0], decays[0] * local_grad[0])
-    state_grad = local_grad + tail_decay * grad_in
-    previous_states = jnp.concatenate([state_in[None], states[:-1]], axis=0)
-    grad_keep, grad_admit, grad_conv_direct, grad_bias_keep, grad_bias_admit, grad_lambda = (
-        piece_back((state_grad * previous_states, state_grad))
-    )
-    keep_low = grad_keep.astype(jnp.bfloat16)
-    admit_low = grad_admit.astype(jnp.bfloat16)
-    gate_blocks_grad = jnp.stack(
-        [block_weight_grad(conv_low, keep_low), block_weight_grad(conv_low, admit_low)]
-    )
-    conv_grad = (
-        grad_conv_direct + block_back(keep_low, gates_low[0]) + block_back(admit_low, gates_low[1])
-    )
+    back_product, local_grad = recurrent_reverse(decays, grad_mixed * branch)
+    factors = [back_product[s * length] for s in range(SEG)]
+    totals = [local_grad[s * length] for s in range(SEG)]
+    factor, total = factors[-1], totals[-1]
+    for s in range(SEG - 2, -1, -1):
+        factor, total = factor * factors[s], totals[s] + factors[s] * total
+    grad_in = entering(decays[0] * factor, decays[0] * total, "seq", True)
+    carries = [grad_in]
+    for s in range(SEG - 1, 0, -1):
+        carries.append(totals[s] + factors[s] * carries[-1])
+    before = jnp.pad(state_in[None], ((7, 0), (0, 0)))
+    conv_grad, keep_paired, admit_paired, gate_sums = gates_backward(
+        conv_low, states, before, back_product, local_grad, jnp.stack(carries[::-1]), rows,
+        keep_blocks, admit_blocks,
+    )
+    gate_blocks_grad = jnp.stack([unpair_blocks(keep_paired), unpair_blocks(admit_paired)])
     edge_grads = passed_along(conv_grad[: CONV - 1], "seq", -1)
-    extended = jnp.concatenate([conv_grad, edge_grads], axis=0)
-    conv_in_grad = jnp.zeros_like(conv_grad)
-    tap_grads = []
-    for tap_index in range(CONV):
-        conv_in_grad = (
-            conv_in_grad + chan_params[tap_index] * extended[tap_index : tap_index + token_count]
-        )
-        tap_grads.append(
-            jnp.sum(
-                conv_grad * padded_in[CONV - 1 - tap_index : CONV - 1 - tap_index + token_count],
-                axis=0,
-            )
-        )
-    conv_bias_grad = jnp.sum(conv_grad, axis=0)
-    conv_in_low = conv_in_grad.astype(jnp.bfloat16)
+    edge_grads = jnp.pad(edge_grads, ((0, 9 - CONV), (0, 0)))
+    conv_in_low, conv_sums = conv_backward(conv_grad, edge_grads, conv_in, edge_rows, rows)
+    lambda_grad = -jax.nn.sigmoid(-chan_params[CONV + 3 :]) * gate_sums[2:3]
     input_weight_grad = contract_rows(hidden_one, conv_in_low)
     branch_weight_grad = contract_rows(hidden_one, branch_grad_low)
     grad_hidden_one = multiply_transposed(conv_in_low, input_weight) + multiply_transposed(
@@ -340,7 +546,7 @@
     input_grad = grad_mid + grad_tokens_norm
     small_terms = (
         jnp.stack([first_gain_grad, second_gain_grad]),
-        jnp.stack(tap_grads + [conv_bias_grad, grad_bias_keep, grad_bias_admit, grad_lambda]),
+        jnp.concatenate([conv_sums[: CONV + 1], gate_sums[:2], lambda_grad], axis=0),
         gate_blocks_grad,
     )
     gains_grad, chan_grad, gates_grad = lax.psum(
@@ -359,6 +565,7 @@
         ),
         tile_of_slot,
         axis=0,
+        mode="clip",
     )
     own_grads = lax.psum_scatter(slot_grads, ("seq", "bat"), scatter_dimension=0, tiled=True)
     soap_out = soap_update(

time: 4740 us -> 1320 us (0.28)
  other arithmetic: 2960 us -> 37.7 us
  local copies, waits for them, and re-layouts: 881 us -> 271 us
  Pallas kernels: 0 us -> 179 us
    another operation x15 -> x3, other arithmetic: 2670 us -> 2.22 us  [the longest x1 1.99 us: on_device(): jnp.stack([unpair_blocks(keep_paired), unpair_blocks(admit_paired)])]
    slice x126 -> x2, local copies, waits for them, and re-layouts: 353 us -> 0.96 us  [the longest x1 0.82 us: on_device(): gate_sums[:2]]
    pallas_call x0 -> x6, Pallas kernels: none -> 179 us  [the longest x2 122 us: chol_qr(): pl.pallas_call(functools.partial(chol_kernel, n, count), out_shape=jax.Sh...]
    pad x64 -> x3, local copies, waits for them, and re-layouts: 178 us -> 0.65 us  [the longest x1 0.63 us: on_device(): before = jnp.pad(state_in[None], ((7, 0), (0, 0)))]
    add x51 -> x9, other arithmetic: 82 us -> 4.37 us  [the longest x8 3.18 us: on_device(): carries.append(totals[s] + factors[s] * carries[-1])]
    select_n x3 -> x2, other arithmetic: 57.4 us -> 0.06 us  [the longest x1 0.04 us: on_device(): jax.nn.softplus(-chan_params[CONV + 3:])]
    rev x2 -> x0, local copies, waits for them, and re-layouts: 49.3 us -> none  [on_device(): lax.associative_scan(combine_pairs, (next_decay, grad_mixed * branch), ax...]
    unnamed x359 -> x161, local copies, waits for them, and re-layouts: 95.2 us -> 89.2 us
  transfers between devices with their start and end apart: 5 -> 5, of which waited for: 2 -> 2; matrix products, arithmetic and copies ran while one was open for 7% -> 21% of each run, Pallas kernels for 0% -> 0%
where the time goes in v1:
time: 1320 us; the launch traced here: 1310 us
  waiting for transfers between devices  548 us (42%)
  local copies, waits for them, and re-layouts  271 us (21%)
  matrix products  195 us (15%)
  Pallas kernels  179 us (14%)
  blocking collectives  56.6 us (4%)
  other arithmetic  37.7 us (3%)
  between operations  15.9 us (1%)
    reduce_scatter x1, waiting for transfers between devices, on_device(): lax.psum_scatter(slot_grads, ('seq', 'bat'), scatter_dimension=0, tiled=T...  398 us
    all_gather x1, waiting for transfers between devices, on_device(): lax.all_gather(tile_weights.astype(jnp.bfloat16), ('seq', 'bat'), axis=0,...  151 us
    pallas_call x2, Pallas kernels, chol_qr(): pl.pallas_call(functools.partial(chol_kernel, n, count), out_shape=jax.Sh...  122 us
    unnamed x161, local copies, waits for them, and re-layouts  89.2 us
    dot_general x6, matrix products, multiply(): return jnp.dot(left_side, matrix, preferred_element_type=jnp.float32)  49.3 us
    psum x1, blocking collectives, on_device(): lax.psum((small_terms[0], small_terms[1], small_terms[2]), ('seq', 'bat'))  41.1 us
    gather x1, local copies, waits for them, and re-layouts, on_device(): jnp.take(join_tiles((input_weight_grad, branch_weight_grad, output_weight...  41 us
    dot_general x6, matrix products, multiply_transposed(): jnp.einsum('tj,ij->ti', left_side, matrix, preferred_element_type=jnp.flo...  33.2 us
  transfers between devices with their start and end apart: 5, of which 2 were waited for; matrix products, arithmetic and copies ran while one was open for 21% of the time, Pallas kernels for 0%

profile of v1, /device:TPU:0, one launch (start us, length us, event | category | flops | bytes accessed | tf_op | source)
XLA Modules:
  0.0 1309.1 jit_solution(15369651896957629158)
XLA Ops:
  14.0 17.0 %scatter_custom_fusion = s32[3456]{0:T(1024)S(1)} fusion(s32[3456]{0:T(1024)S(1)} %compare_select_fusion, s32[3456]{0:T(1024)S(1)} %iota.8, s32[]{:T(128)} %constant.30.clone.1), kind=kCustom, calls=%fused_computation.188 | custom fusion | bytes 13828 | tf_op jit(solution)/shard_map/scatter | solution.py:462
  33.3 150.8 %all-gather.6.cloned.1.call-done = bf16[3456,32,128]{2,1,0:T(8,128)(2,1)} async-done(((bf16[108,32,128]{2,1,0:T(8,128)(2,1)}), bf16[3456,32,128]{2,1,0:T(8,128)(2,1)}) %all-gather.6.cloned.1.call-update) | async-done | bytes 28311568 | tf_op jit(solution)/shard_map/all_gather | solution.py:457
  184.1 21.9 %gather_fusion = bf16[3456,32,128]{2,1,0:T(8,128)(2,1)} fusion(bf16[3456,32,128]{2,1,0:T(8,128)(2,1)} %all-gather.6.cloned.1.call-done, s32[4096]{0:T(1024)S(1)} %pad_clamp_fusion.1), kind=kCustom, calls=%fused_computation | custom fusion | bytes 56636928 | tf_op jit(solution)/shard_map/jit(_take)/gather | solution.py:465
  212.4 11.3 fusion.133
  232.6 11.8 copy.85
  244.4 9.7 fusion.16
  272.5 19.4 %recurrence_forward.1 = (bf16[512,1536]{1,0:T(8,128)(2,1)S(1)}, f32[512,1536]{1,0:T(8,128)}, f32[512,1536]{1,0:T(8,128)}, f32[512,1536]{1,0:T(8,128)}) custom-call(f32[512,1536]{1,0:T(8,128)} %copy-done.16, f32[8,1536]{1,0:T(8,128)S(1)} %pad.16.edge_ref.before_ref, f32[8,1536]{1,0:T(8,128)S(1)} %pad_maximum_fusion.3.rows_ref, ...), custom_call_target="tpu_custom_call" | custom-call | tf_op jit(solution)/shard_map/recurrence_forward/pallas_call | solution.py:134
  295.4 8.2 all-gather.2
  312.2 9.2 multiply_convert_fusion.3
  332.0 13.5 %fusion.6 = (bf16[512,3072]{1,0:T(8,128)(2,1)}, bf16[512,3072]{1,0:T(8,128)(2,1)}, f32[512,3072]{1,0:T(8,128)}) fusion(f32[512,3072]{1,0:T(8,128)} %fusion.16, f32[512,3072]{1,0:T(8,128)} %fusion.22, bf16[512,1024]{1,0:T(8,128)(2,1)S(1)} %multiply_convert_fusion.6, bf16[128,8,24,128]{3,2,1,0:T(8,128)(2,1)S(1)} %bitcast.395), kind=kOutput, calls=%fused_computation.13 | convolution fusion | flops 3258974208 | bytes 32505856 | tf_op jit(solution)/shard_map/dot_general | solution.py:56
  383.1 16.9 %recurrence_reverse.1 = (f32[512,1536]{1,0:T(8,128)S(1)}, f32[512,1536]{1,0:T(8,128)}) custom-call(f32[512,1536]{1,0:T(8,128)} %get-tuple-element.33.decays_ref, f32[512,1536]{1,0:T(8,128)} %get-tuple-element.145.source_ref), custom_call_target="tpu_custom_call" | custom-call | tf_op jit(solution)/shard_map/recurrence_reverse/pallas_call | solution.py:176
  402.1 7.2 all-gather.3
  411.1 15.0 %gates_backward.1 = (f32[512,1536]{1,0:T(8,128)}, f32[4,384,384]{2,1,0:T(8,128)}, f32[4,384,384]{2,1,0:T(8,128)}, f32[8,1536]{1,0:T(8,128)}) custom-call(bf16[512,1536]{1,0:T(8,128)(2,1)} %copy-done.4, f32[512,1536]{1,0:T(8,128)} %copy-done.19, f32[8,1536]{1,0:T(8,128)} %pad.17.before_ref, f32[512,1536]{1,0:T(8,128)} %copy-done.2, ...), custom_call_target="tpu_custom_call" | custom-call | tf_op jit(solution)/shard_map/gates_backward/pallas_call | solution.py:228
  444.2 8.6 fusion.139
  467.5 12.2 copy.120
  479.7 11.5 copy.92
  491.2 12.1 copy.121
  503.3 11.8 copy.93
  545.1 11.1 constant_dynamic-update-slice_fusion.2
  556.1 10.9 constant_dynamic-update-slice_fusion.1
  567.0 10.7 constant_dynamic-update-slice_fusion
  577.6 41.0 %gather_fusion.1 = f32[3456,32,128]{2,1,0:T(8,128)} fusion(f32[3456,32,128]{2,1,0:T(8,128)} %constant_dynamic-update-slice_fusion, s32[4096]{0:T(1024)S(1)} %copy-done.49), kind=kCustom, calls=%fused_computation.1 | custom fusion | bytes 113260032 | tf_op jit(solution)/shard_map/jit(_take)/gather | solution.py:555
  626.5 17.6 %add_bitcast_fusion = f32[1,512,1024]{2,1,0:T(8,128)} fusion(f32[512,1024]{1,0:T(8,128)} %copy-done.21, bf16[384,8,8,128]{3,2,1,0:T(8,128)(2,1)} %bitcast.392, f32[512,3072]{1,0:T(8,128)} %fusion.22, f32[512,3072]{1,0:T(8,128)} %get-tuple-element.168), kind=kOutput, calls=%fused_computation.107 | convolution fusion | flops 3237478400 | bytes 23068672 | tf_op jit(solution)/shard_map/dot_general | solution.py:56
  644.1 41.1 %all-reduce.7 = (f32[2,1024]{1,0:T(2,128)S(1)}, f32[8,1536]{1,0:T(8,128)S(1)}) all-reduce(f32[2,1024]{1,0:T(2,128)S(1)} %pad_maximum_fusion.5, f32[8,1536]{1,0:T(8,128)S(1)} %pad_maximum_fusion.4), channel_id=1, replica_groups=mesh['seq'=4,'bat'=8] {'seq','bat'}, use_global_device_ids=true, to_apply=%region_7.8 | all-reduce | flops 14336 | bytes 114688 | tf_op jit(solution)/shard_map/psum | solution.py:552
  686.6 8.6 multiply_subtract_fusion
  695.2 397.5 %reduce-scatter.2.cloned.1.call-done = f32[108,32,128]{2,1,0:T(8,128)} async-done(((f32[3456,32,128]{2,1,0:T(8,128)}), f32[108,32,128]{2,1,0:T(8,128)}) %reduce-scatter.2.cloned.1.call-update) | async-done | bytes 1769488 | tf_op jit(solution)/shard_map/reduce_scatter | solution.py:570
  1122.1 12.5 multiply_subtract_fusion.1
  1138.9 18.1 %shard_map.331 = f32[3456,32]{1,0:T(8,128)} custom-call(f32[3456,32]{1,0:T(8,128)} %bitcast.390, f32[3456,32]{1,0:T(8,128)} %bitcast.373), custom_call_target="tpu_custom_call" | custom-call | tf_op jit(solution)/shard_map/pallas_call | solution.py:381
  1160.2 14.4 %multiply_add_fusion = f32[108,128,128]{2,1,0:T(8,128)S(1)} fusion(f32[108,128,128]{2,1,0:T(8,128)} %param.38, f32[108,32,128]{2,1,0:T(8,128)} %reduce-scatter.2.cloned.1.call-done), kind=kOutput, calls=%fused_computation.6 | convolution fusion | flops 684785664 | bytes 15925248 | tf_op jit(solution)/shard_map/nji,njk->nik/dot_general | solution.py:411
  1174.6 9.5 fusion.143
  1184.2 14.4 %fusion.144 = f32[108,128,128]{2,1,0:T(8,128)} fusion(f32[108,128,128]{2,1,0:T(8,128)S(1)} %fusion.143), kind=kOutput, calls=%fused_computation.265 | convolution fusion | flops 2717908992 | bytes 14155776 | tf_op jit(solution)/shard_map/nij,nik->njk/dot_general | solution.py:393
  1198.5 103.6 %shard_map.332 = f32[13824,128]{1,0:T(8,128)} custom-call(f32[13824,128]{1,0:T(8,128)} %bitcast.374, f32[13824,128]{1,0:T(8,128)} %bitcast.364), custom_call_target="tpu_custom_call" | custom-call | tf_op jit(solution)/shard_map/pallas_call | solution.py:381
  (264 shorter events, 214.2 us)
Async XLA Ops:
  7.2 176.9 %all-gather.6.cloned.1.call-start = ((), (), s32[]{:S(2)}) async-start(), calls=%async_computation.1 | async-start | bytes 29196288 | tf_op jit(solution)/shard_map/all_gather | solution.py:457
  9.8 21.8 %copy-start.10 = (f32[1,512,1024]{2,1,0:T(8,128)S(1)}, f32[1,512,1024]{2,1,0:T(8,128)}, u32[]{:S(2)}) copy-start(f32[1,512,1024]{2,1,0:T(8,128)} %param.20) | copy-start | bytes 6291460
  9.8 676.7 %all-reduce.10.cloned.1.call-start = ((), (), s32[]{:S(2)}) async-start(), calls=%async_computation.2 | async-start | bytes 6291456 | tf_op jit(solution)/shard_map/psum | solution.py:552
  9.9 22.5 %copy-start.52 = (f32[2,1024]{1,0:T(2,128)S(1)}, f32[2,1024]{1,0:T(2,128)}, u32[]{:S(2)}) copy-start(f32[2,1024]{1,0:T(2,128)} %param.23) | copy-start | bytes 24580
  9.9 22.5 %copy-start.46 = (f32[8,1536]{1,0:T(8,128)S(1)}, f32[8,1536]{1,0:T(8,128)}, u32[]{:S(2)}) copy-start(f32[8,1536]{1,0:T(8,128)} %param.24) | copy-start | bytes 147460
  32.5 239.9 %copy-start.5 = (f32[8,1536]{1,0:T(8,128)}, f32[8,1536]{1,0:T(8,128)S(1)}, u32[]{:S(2)}) copy-start(f32[8,1536]{1,0:T(8,128)S(1)} %pad_maximum_fusion.3.rows_ref) | copy-start | bytes 147460
  33.3 239.1 %copy-start = (bf16[4,384,384]{2,1,0:T(8,128)(2,1)}, bf16[4,384,384]{2,1,0:T(8,128)(2,1)S(1)}, u32[]{:S(2)}) copy-start(bf16[4,384,384]{2,1,0:T(8,128)(2,1)S(1)} %get-tuple-element.171.keep_ref) | copy-start | bytes 3538948
  33.3 239.1 %copy-start.1 = (bf16[4,384,384]{2,1,0:T(8,128)(2,1)}, bf16[4,384,384]{2,1,0:T(8,128)(2,1)S(1)}, u32[]{:S(2)}) copy-start(bf16[4,384,384]{2,1,0:T(8,128)(2,1)S(1)} %get-tuple-element.172.admit_ref) | copy-start | bytes 3538948
  229.0 43.4 %collective-permute-start = (f32[3,1536]{1,0:T(4,128)S(1)}, f32[3,1536]{1,0:T(4,128)S(1)}, u32[]{:S(2)}, u32[]{:S(2)}) collective-permute-start(f32[3,1536]{1,0:T(4,128)S(1)} %slice.303), channel_id=1, source_target_pairs={{0,8},{8,16},{16,24},{1,9},{9,17},{17,25},{2,10},{10,18},{18,26},{... | collective-permute-start | bytes 55304 | tf_op jit(solution)/shard_map/ppermute | solution.py:52
  244.4 9.7 copy-start.17
  293.0 19.2 %copy-start.12 = (f32[1,512,1024]{2,1,0:T(8,128)S(1)}, f32[1,512,1024]{2,1,0:T(8,128)}, u32[]{:S(2)}) copy-start(f32[1,512,1024]{2,1,0:T(8,128)} %param.20) | copy-start | bytes 6291460
  321.4 50.2 %copy-start.19 = (f32[512,1536]{1,0:T(8,128)}, f32[512,1536]{1,0:T(8,128)S(1)}, u32[]{:S(2)}) copy-start(f32[512,1536]{1,0:T(8,128)S(1)} %get-tuple-element.129.states_ref) | copy-start | bytes 9437188
  323.3 46.6 %copy-start.21 = (f32[512,1024]{1,0:T(8,128)}, f32[512,1024]{1,0:T(8,128)S(1)}, u32[]{:S(2)}) copy-start(f32[512,1024]{1,0:T(8,128)S(1)} %get-tuple-element.167) | copy-start | bytes 6291460
  400.0 11.1 copy-start.2
  426.9 88.2 %collective-permute-start.1 = (f32[3,1536]{1,0:T(4,128)S(1)}, f32[3,1536]{1,0:T(4,128)S(1)}, u32[]{:S(2)}, u32[]{:S(2)}) collective-permute-start(f32[3,1536]{1,0:T(4,128)S(1)} %slice.290), channel_id=1, source_target_pairs={{8,0},{16,8},{24,16},{9,1},{17,9},{25,17},{10,2},{18,10},{26,18},{... | collective-permute-start | bytes 55304 | tf_op jit(solution)/shard_map/ppermute | solution.py:52
  434.1 658.5 %reduce-scatter.2.cloned.1.call-start = ((), (), s32[]{:S(2)}) async-start(), calls=%async_computation.3 | async-start | bytes 58392576 | tf_op jit(solution)/shard_map/reduce_scatter | solution.py:570
  503.3 11.8 copy-start.3
  503.3 11.8 copy-start.6
  567.0 10.7 copy-start.49
  626.4 17.6 %copy-start.58 = (f32[1024]{0:T(1024)S(1)}, f32[1024]{0:T(1024)}, u32[]{:S(2)}) copy-start(f32[1024]{0:T(1024)} %get-tuple-element.98) | copy-start | bytes 12292
  626.4 58.8 %copy-start.53 = (f32[2,1024]{1,0:T(2,128)S(1)}, f32[2,1024]{1,0:T(2,128)}, u32[]{:S(2)}) copy-start(f32[2,1024]{1,0:T(2,128)} %param.23) | copy-start | bytes 24580
  626.4 58.8 %copy-start.56 = (f32[2,1024]{1,0:T(2,128)S(1)}, f32[2,1024]{1,0:T(2,128)}, u32[]{:S(2)}) copy-start(f32[2,1024]{1,0:T(2,128)} %param.27) | copy-start | bytes 24580
  626.5 58.8 %copy-start.57 = (f32[2,1024]{1,0:T(2,128)S(1)}, f32[2,1024]{1,0:T(2,128)}, u32[]{:S(2)}) copy-start(f32[2,1024]{1,0:T(2,128)} %param.26) | copy-start | bytes 24580
  626.5 59.4 %copy-start.50 = (f32[8,1536]{1,0:T(8,128)S(1)}, f32[8,1536]{1,0:T(8,128)}, u32[]{:S(2)}) copy-start(f32[8,1536]{1,0:T(8,128)} %param.29) | copy-start | bytes 147460
  626.5 59.4 %copy-start.51 = (f32[8,1536]{1,0:T(8,128)S(1)}, f32[8,1536]{1,0:T(8,128)}, u32[]{:S(2)}) copy-start(f32[8,1536]{1,0:T(8,128)} %param.28) | copy-start | bytes 147460
  626.5 60.1 %copy-start.20 = (f32[2,8,192,192]{3,2,1,0:T(8,128)S(1)}, f32[2,8,192,192]{3,2,1,0:T(8,128)}, u32[]{:S(2)}) copy-start(f32[2,8,192,192]{3,2,1,0:T(8,128)} %param.25) | copy-start | bytes 7077892
  1092.7 19.7 %slice-start = ((s8[7077888]{0:T(1024)(128)(4,1)}), s8[2883584]{0:T(1024)(128)(4,1)S(1)}, s32[]{:S(2)}) async-start(s8[7077888]{0:T(1024)(128)(4,1)} %bitcast.365), calls=%async_computation.4 | async-start | bytes 5767168
  1102.7 9.7 slice-start.1
  1106.7 27.9 %copy-start.9 = (f32[108,32,32]{2,1,0:T(8,128)}, f32[108,32,32]{2,1,0:T(8,128)S(1)}, u32[]{:S(2)}) copy-start(f32[108,32,32]{2,1,0:T(8,128)S(1)} %fusion.141) | copy-start | bytes 1327108
  1138.9 35.7 %slice-start.2 = ((s8[7077888]{0:T(1024)(128)(4,1)}), s8[2883584]{0:T(1024)(128)(4,1)S(1)}, s32[]{:S(2)}) async-start(s8[7077888]{0:T(1024)(128)(4,1)} %bitcast.367), calls=%async_computation.6 | async-start | bytes 5767168
  1160.2 14.4 %slice-start.3 = ((s8[7077888]{0:T(1024)(128)(4,1)}), s8[4194304]{0:T(1024)(128)(4,1)S(1)}, s32[]{:S(2)}) async-start(s8[7077888]{0:T(1024)(128)(4,1)} %bitcast.367), calls=%async_computation.7 | async-start | bytes 8388608
  1184.1 14.4 %copy-start.7 = (f32[108,128,128]{2,1,0:T(8,128)}, f32[108,128,128]{2,1,0:T(8,128)S(1)}, u32[]{:S(2)}) copy-start(f32[108,128,128]{2,1,0:T(8,128)S(1)} %fusion.143) | copy-start | bytes 21233668
  (44 other events, 197.8 us)
Sparse Core Ops, SparseCore 0:
  11.6 172.4 all-gather.5
  434.2 137.9 all-reduce.9
  618.9 473.7 reduce-scatter.1
